TPU v7x, 32 devices: a whole 2x2x4 slice. The times are simulated.
32 devices in a mesh: replica: 2 (over y), dev: 8 (over z, x), pair: 2 (over core).
Axes of the slice: x: 2, y: 2, z: 4, core: 2. Of those that a mesh axis runs over, the one named last changes fastest.
Arguments:
- text_rows: bfloat16 [2048, 8192], P(('replica', 'dev'), 'pair'), parts along dimension 0, may hold values from -6 to 6
- vision_rows: bfloat16 [1024, 8192], P(('replica', 'dev'), 'pair'), parts along dimension 0, may hold values from -6 to 6
- vision_device: int32 [1024, 1], P(('replica', 'dev')), parts along dimension 0, may hold values from 0 to 7; in each aligned block of 64 rows (0 to 63, 64 to 127, ...) at most 16 rows name the same one
- vision_slot: int32 [1024], P(('replica', 'dev')), parts along dimension 0, may hold values from 0 to 127
- positions: int32 [2048], P(('replica', 'dev')), parts along dimension 0, may hold values from 0 to 1023, each once
- norm_gain: bfloat16 [8192], replicated, may hold values from 0.099609375 to 1.8984375
- kv_weight: bfloat16 [8192, 1024], P('dev', 'pair'), may hold values from -0.0625 to 0.0625
- kv_bias: bfloat16 [1024], P('pair'), may hold values from -3 to 3
- queries: bfloat16 [2048, 4096], P(('replica', 'dev'), 'pair'), parts along dimension 0
- page_table: int32 [16, 8], P(('replica', 'dev')), parts along dimension 0, may hold values from 0 to 7, each once within a row
Outputs:
- attended: bfloat16 [2048, 4096], P(('replica', 'dev'), 'pair'), parts along dimension 0
- kv_cache: bfloat16 [128, 16, 1024], P(('replica', 'dev'), None, 'pair'), parts along dimension 0
There are 2 independent parts, one for each index of `replica`. A program takes and returns all parts, laid end to end along the dimension named above; an argument that names none is the same for every part. Nothing has to cross between parts.
Inputs may be any that keep to these rules, and one draw needn't show every extreme that they name: `vision_device`: among the vision rows of one index of dev at most 16 name the same index. `positions`: each prompt position appears once. `page_table`: each row names each of its 8 pages once.
All inputs are finite; a program needn't handle non-finite values.
Results may differ from a plain program's by a relative error of at most 0.0039.
The roundings to bfloat16 on the way count: a program that leaves them out, or rounds other values in their place, can miss the bound.
Values may be sent and summed in bfloat16 or wider, within the bound.
A program may use at most 64 MiB of HBM per device.

v0:
```python
import math

import jax
import jax.numpy as jnp
from jax import lax
from jax.sharding import PartitionSpec as P

HD = 128
PAGE = 16


def score_block(carry, keys_part, key_pos, query, query_pos):
    peak, total, mixed = carry
    heads = query.shape[1]
    split = keys_part.reshape(keys_part.shape[0], heads, 2, -1)
    keys = split[:, :, 0]
    values = split[:, :, 1]
    scores = jnp.einsum(
        "tkgd,skd->kgts", query, keys, preferred_element_type=jnp.float32
    ) * query.shape[3] ** (-0.5)
    allowed = key_pos[None, :] <= query_pos[:, None]
    scores = jnp.where(allowed, scores, -1e30)
    new_peak = jnp.maximum(peak, jnp.max(scores, axis=-1))
    weights = jnp.where(allowed, jnp.exp(scores - new_peak[..., None]), 0.0)
    factor = jnp.exp(peak - new_peak)
    total = total * factor + jnp.sum(weights, axis=-1)
    mixed = mixed * factor[..., None] + jnp.einsum(
        "kgts,skd->kgtd", weights.astype(jnp.bfloat16), values, preferred_element_type=jnp.float32
    )
    return (new_peak, total, mixed)


def local(
    text_rows,
    vision_rows,
    vision_device,
    vision_slot,
    positions,
    norm_gain,
    kv_weight,
    kv_bias,
    queries,
    page_table,
):
    n_dev = lax.axis_size("dev")
    tok = text_rows.shape[0]
    nvis = vision_rows.shape[0]
    cap = max(2, 2 * nvis // n_dev)
    dest = vision_device[:, 0]
    onehot = (dest[:, None] == jnp.arange(n_dev, dtype=jnp.int32)[None, :]).astype(jnp.int32)
    rank = jnp.sum((jnp.cumsum(onehot, axis=0) - 1) * onehot, axis=1)
    slot_index = dest * cap + rank
    select = jnp.arange(n_dev * cap, dtype=jnp.int32)[:, None] == slot_index[None, :]
    send_rows = jnp.dot(
        select.astype(jnp.bfloat16), vision_rows, preferred_element_type=jnp.float32
    ).astype(jnp.bfloat16)
    send_rows = send_rows.reshape(n_dev, cap, -1)
    send_slots = jnp.max(jnp.where(select, vision_slot[None, :], -1), axis=1).reshape(n_dev, cap)
    recv_rows, recv_slots = (
        lax.all_to_all(send_rows, "dev", split_axis=0, concat_axis=0, tiled=True),
        lax.all_to_all(send_slots, "dev", split_axis=0, concat_axis=0, tiled=True),
    )
    placing = (jnp.arange(tok, dtype=jnp.int32)[:, None] == recv_slots.reshape(1, -1)).astype(
        jnp.bfloat16
    )
    added = jnp.dot(placing, recv_rows.reshape(n_dev * cap, -1), preferred_element_type=jnp.float32)
    embedded = (text_rows.astype(jnp.float32) + added).astype(jnp.bfloat16)
    whole = lax.all_gather(embedded, "pair", axis=1, tiled=True)
    floats = whole.astype(jnp.float32)
    meansq = jnp.mean(floats * floats, axis=-1, keepdims=True)
    normed = (floats * lax.rsqrt(meansq + 1e-06) * norm_gain.astype(jnp.float32)).astype(
        jnp.bfloat16
    )
    projected = jnp.dot(
        normed,
        lax.all_gather(kv_weight, "dev", axis=0, tiled=True),
        preferred_element_type=jnp.float32,
    )
    kv = (projected + kv_bias.astype(jnp.float32)).astype(jnp.bfloat16)
    kv_cache = jnp.take(kv.reshape(-1, PAGE, kv.shape[1]), page_table[0], axis=0)
    kv_heads = kv.shape[1] // (2 * HD)
    group = queries.shape[1] // (HD * kv_heads)
    query = queries.reshape(tok, kv_heads, group, HD)
    start_state = (
        jnp.full((kv_heads, group, tok), -1e30, jnp.float32),
        jnp.zeros((kv_heads, group, tok), jnp.float32),
        jnp.zeros((kv_heads, group, tok, HD), jnp.float32),
    )
    keys_part = lax.all_gather(kv, "dev", axis=0, tiled=True)
    key_pos = lax.all_gather(positions, "dev", axis=0, tiled=True)
    rows = keys_part.shape[0]
    block = math.gcd(rows, 512)
    keys_blocks = keys_part.reshape(rows // block, block, -1)
    pos_blocks = key_pos.reshape(rows // block, block)

    def step(state, item):
        return (score_block(state, item[0], item[1], query, positions), None)

    result, unused = lax.scan(step, start_state, (keys_blocks, pos_blocks))
    peak, total, mixed = result
    mixed = mixed / total[..., None]
    attended = jnp.transpose(mixed, (2, 0, 1, 3)).reshape(tok, -1).astype(jnp.bfloat16)
    return (attended, kv_cache)


def solution(mesh):
    placed = (
        P(("replica", "dev"), "pair"),
        P(("replica", "dev"), "pair"),
        P(("replica", "dev"), None),
        P(("replica", "dev")),
        P(("replica", "dev")),
        P(),
        P("dev", "pair"),
        P("pair"),
        P(("replica", "dev"), "pair"),
        P(("replica", "dev"), None),
    )
    return jax.shard_map(
        local,
        mesh=mesh,
        in_specs=placed,
        out_specs=(P(("replica", "dev"), "pair"), P(("replica", "dev"), None, "pair")),
        check_vma=False,
    )
```

profile of v0, /device:TPU:0, one launch (start us, length us, event | category | flops | bytes accessed | tf_op | source)
XLA Modules:
  0.0 263.9 jit_solution(137521374386064671)
XLA Ops:
  7.2 0.8 fusion.30
  8.1 0.8 select_reduce_fusion.1
  9.0 0.7 multiply_add_fusion
  9.6 0.7 select_reduce_fusion
  10.4 0.7 all_to_all.9
  11.1 7.3 %all-to-all-start = ((s32[8,1,16]{2,1,0:T(1,128)}), s32[8,1,16]{2,1,0:T(1,128)S(1)}, u32[]{:S(2)}, u32[]{:S(2)}) async-start(s32[8,1,16]{2,1,0:T(1,128)} %bitcast.2), calls=%async_computation | async-start | bytes 8192 | tf_op jit(solution)/shard_map/all_to_all | solution.py:61
  18.3 1.5 convolution_convert_fusion
  19.9 4.8 %all-to-all-done = s32[8,1,16]{2,1,0:T(1,128)S(1)} async-done(((s32[8,1,16]{2,1,0:T(1,128)}), s32[8,1,16]{2,1,0:T(1,128)S(1)}, u32[]{:S(2)}, u32[]{:S(2)}) %all-to-all-start) | async-done | bytes 544 | tf_op jit(solution)/shard_map/all_to_all | solution.py:61
  24.7 3.6 %all-to-all-start.1 = ((bf16[8,16,4096]{2,1,0:T(8,128)(2,1)}), bf16[8,16,4096]{2,1,0:T(8,128)(2,1)S(1)}, u32[]{:S(2)}, u32[]{:S(2)}) async-start(bf16[8,16,4096]{2,1,0:T(8,128)(2,1)} %bitcast.3), calls=%async_computation.1 | async-start | bytes 2097152 | tf_op jit(solution)/shard_map/all_to_all | solution.py:60
  28.8 0.7 reduce.7
  29.6 23.4 %all-to-all-done.1 = bf16[8,16,4096]{2,1,0:T(8,128)(2,1)S(1)} async-done(((bf16[8,16,4096]{2,1,0:T(8,128)(2,1)}), bf16[8,16,4096]{2,1,0:T(8,128)(2,1)S(1)}, u32[]{:S(2)}, u32[]{:S(2)}) %all-to-all-start.1) | async-done | bytes 1048608 | tf_op jit(solution)/shard_map/all_to_all | solution.py:60
  53.0 1.4 fusion.14
  54.5 0.7 all-gather.7.cloned.1.call-update
  55.3 8.8 %all-gather.5.cloned.1.call-done = bf16[128,8192]{1,0:T(8,128)(2,1)} async-done(((bf16[128,4096]{1,0:T(8,128)(2,1)}), bf16[128,8192]{1,0:T(8,128)(2,1)}) %all-gather.5.cloned.1.call-update) | async-done | bytes 2097168 | tf_op jit(solution)/shard_map/all_gather | solution.py:68
  64.1 2.1 fusion.15
  66.2 126.1 %all-gather.7.cloned.1.call-done = bf16[8192,512]{1,0:T(8,128)(2,1)} async-done(((bf16[1024,512]{1,0:T(8,128)(2,1)}), bf16[8192,512]{1,0:T(8,128)(2,1)}) %all-gather.7.cloned.1.call-update) | async-done | bytes 8388624 | tf_op jit(solution)/shard_map/all_gather | solution.py:76
  192.3 6.0 %fusion.25 = bf16[128,512]{1,0:T(8,128)(2,1)} fusion(bf16[8192,512]{1,0:T(8,128)(2,1)} %all-gather.7.cloned.1.call-done, bf16[128,8192]{1,0:T(8,128)(2,1)} %all-gather.5.cloned.1.call-done, f32[8192]{0:T(1024)S(1)} %convert_element_type.46, f32[128]{0:T(128)S(1)} %add_rsqrt_fusion, f32[512]{0:T(512)S(1)} %convert_element_type.48), kind=kOutput, calls=%fused_computation.35 | convolution fusion | flops 1078067200 | bytes 10652160 | tf_op jit(solution)/shard_map/dot_general | solution.py:74
  198.4 17.5 %all-gather = s32[8,1,128]{2,1,0:T(1,128)S(1)} all-gather(s32[1,1,128]{2,1,0:T(1,128)S(1)} %bitcast.82), channel_id=1, replica_groups=mesh['replica'=2,'dev'=8,'pair'=2] {'dev'}, dimensions={0}, use_global_device_ids=true | all-gather | bytes 4608 | tf_op jit(solution)/shard_map/all_gather | solution.py:90
  215.8 0.7 reduce.6
  217.1 1.5 gather_fusion
  218.6 0.7 broadcast_select_fusion
  219.3 17.5 %all-gather.9.cloned.1.call-done = bf16[1024,512]{1,0:T(8,128)(2,1)} async-done(((bf16[128,512]{1,0:T(8,128)(2,1)}), bf16[1024,512]{1,0:T(8,128)(2,1)}) %all-gather.9.cloned.1.call-update) | async-done | bytes 1048592 | tf_op jit(solution)/shard_map/all_gather | solution.py:89
  236.9 18.9 %while.15 = (s32[]{:T(128)}, f32[2,8,128]{2,1,0:T(8,128)S(1)}, f32[2,8,128]{2,1,0:T(8,128)S(1)}, f32[2,8,128,128]{3,2,1,0:T(8,128)S(1)}, s32[2,512]{1,0:T(2,128)...) while((s32[]{:T(128)}, f32[2,8,128]{2,1,0:T(8,128)S(1)}, ...), condition=%wide.region_7.8_spmd.clone, body=%wide.region_4.7_spmd.clone.sunk | while | flops 551364608 | bytes 35003028 | solution.py:99
  237.0 1.1 constant_dynamic-slice_fusion.5
  238.3 2.8 %fusion.45 = (f32[2,8,128]{2,1,0:T(8,128)S(1)}, f32[2,512,128,8]{2,1,3,0:T(8,128)}) fusion(pred[128,512]{0,1:T(8,128)(4,1)S(1)} %broadcast_compare_fusion.2, bf16[128,2,8,128]{3,0,2,1:T(8,128)(2,1)S(1)} %get-tuple-element.202, bf16[512,2,2,128]{0,3,2,1:T(8,128)(2,1)S(1)} %bitcast.73), kind=kOutput, calls=%fused_computation.3.clone.1 | convolution fusion | flops 271579136 | bytes 5054464 | tf_op jit(solution)/shard_map/while/body/eval_jaxpr/tkgd,skd->kgts/dot_general | solution.py:18
  241.1 3.3 %fusion.46 = f32[2,8,128]{2,1,0:T(8,128)S(1)} fusion(f32[2,512,128,8]{2,1,3,0:T(8,128)} %get-tuple-element.172, f32[2,8,128]{2,1,0:T(8,128)S(1)} %select_maximum_fusion.2, pred[128,512]{0,1:T(8,128)(4,1)S(1)} %broadcast_compare_fusion.2), kind=kLoop, calls=%fused_computation.5.clone.1 | loop fusion | flops 5240832 | bytes 4276224 | tf_op jit(solution)/shard_map/while/body/eval_jaxpr/reduce_sum | solution.py:26
  244.6 1.7 fusion.48
  246.5 1.1 constant_dynamic-slice_fusion.5
  247.8 2.8 %fusion.45 = (f32[2,8,128]{2,1,0:T(8,128)S(1)}, f32[2,512,128,8]{2,1,3,0:T(8,128)}) fusion(pred[128,512]{0,1:T(8,128)(4,1)S(1)} %broadcast_compare_fusion.2, bf16[128,2,8,128]{3,0,2,1:T(8,128)(2,1)S(1)} %get-tuple-element.202, bf16[512,2,2,128]{0,3,2,1:T(8,128)(2,1)S(1)} %bitcast.73), kind=kOutput, calls=%fused_computation.3.clone.1 | convolution fusion | flops 271579136 | bytes 5054464 | tf_op jit(solution)/shard_map/while/body/eval_jaxpr/tkgd,skd->kgts/dot_general | solution.py:18
  250.6 3.3 %fusion.46 = f32[2,8,128]{2,1,0:T(8,128)S(1)} fusion(f32[2,512,128,8]{2,1,3,0:T(8,128)} %get-tuple-element.172, f32[2,8,128]{2,1,0:T(8,128)S(1)} %select_maximum_fusion.2, pred[128,512]{0,1:T(8,128)(4,1)S(1)} %broadcast_compare_fusion.2), kind=kLoop, calls=%fused_computation.5.clone.1 | loop fusion | flops 5240832 | bytes 4276224 | tf_op jit(solution)/shard_map/while/body/eval_jaxpr/reduce_sum | solution.py:26
  254.0 1.7 fusion.48
  256.5 0.9 copy.45
  (52 shorter events, 3.1 us)
Async XLA Ops:
  7.2 11.2 %copy-start = (bf16[64,4096]{1,0:T(8,128)(2,1)S(1)}, bf16[64,4096]{1,0:T(8,128)(2,1)}, u32[]{:S(2)}) copy-start(bf16[64,4096]{1,0:T(8,128)(2,1)} %param.13) | copy-start | bytes 1572868
  7.2 45.8 %copy-start.2 = (bf16[128,4096]{1,0:T(8,128)(2,1)S(1)}, bf16[128,4096]{1,0:T(8,128)(2,1)}, u32[]{:S(2)}) copy-start(bf16[128,4096]{1,0:T(8,128)(2,1)} %param.12) | copy-start | bytes 3145732
  11.1 13.6 %all-to-all-start = ((s32[8,1,16]{2,1,0:T(1,128)}), s32[8,1,16]{2,1,0:T(1,128)S(1)}, u32[]{:S(2)}, u32[]{:S(2)}) async-start(s32[8,1,16]{2,1,0:T(1,128)} %bitcast.2), calls=%async_computation | async-start | bytes 8192 | tf_op jit(solution)/shard_map/all_to_all | solution.py:61
  18.3 36.9 %copy-start.5 = (bf16[8192]{0:T(1024)(128)(2,1)S(1)}, bf16[8192]{0:T(1024)(128)(2,1)}, u32[]{:S(2)}) copy-start(bf16[8192]{0:T(1024)(128)(2,1)} %param.17) | copy-start | bytes 49156
  18.3 36.9 %copy-start.6 = (bf16[512]{0:T(512)(128)(2,1)S(1)}, bf16[512]{0:T(512)(128)(2,1)}, u32[]{:S(2)}) copy-start(bf16[512]{0:T(512)(128)(2,1)} %param.19) | copy-start | bytes 3076
  24.7 28.3 %all-to-all-start.1 = ((bf16[8,16,4096]{2,1,0:T(8,128)(2,1)}), bf16[8,16,4096]{2,1,0:T(8,128)(2,1)S(1)}, u32[]{:S(2)}, u32[]{:S(2)}) async-start(bf16[8,16,4096]{2,1,0:T(8,128)(2,1)} %bitcast.3), calls=%async_computation.1 | async-start | bytes 2097152 | tf_op jit(solution)/shard_map/all_to_all | solution.py:60
  28.3 35.8 %all-gather.5.cloned.1.call-start = ((), (), s32[]{:S(2)}) async-start(), calls=%async_computation.2 | async-start | bytes 3145728 | tf_op jit(solution)/shard_map/all_gather | solution.py:68
  54.4 137.9 %all-gather.7.cloned.1.call-start = ((), (), s32[]{:S(2)}) async-start(), calls=%async_computation.3 | async-start | bytes 9437184 | tf_op jit(solution)/shard_map/all_gather | solution.py:76
  55.2 181.7 %all-gather.9.cloned.1.call-start = ((), (), s32[]{:S(2)}) async-start(), calls=%async_computation.4 | async-start | bytes 1179648 | tf_op jit(solution)/shard_map/all_gather | solution.py:89
  66.1 132.2 %copy-start.4 = (s32[128]{0:T(128)S(1)}, s32[128]{0:T(128)}, u32[]{:S(2)}) copy-start(s32[128]{0:T(128)} %param.16) | copy-start | bytes 1540
  66.2 150.4 %copy-start.3 = (bf16[128,2048]{1,0:T(8,128)(2,1)S(1)}, bf16[128,2048]{1,0:T(8,128)(2,1)}, u32[]{:S(2)}) copy-start(bf16[128,2048]{1,0:T(8,128)(2,1)} %param.20) | copy-start | bytes 1572868
  66.2 150.9 %copy-start.7 = (s32[1,8]{1,0:T(1,128)S(1)}, s32[1,8]{1,0:T(1,128)}, u32[]{:S(2)}) copy-start(s32[1,8]{1,0:T(1,128)} %param.21) | copy-start | bytes 100
  241.1 3.4 %copy-start.1 = (f32[2,512,128,8]{2,1,3,0:T(8,128)S(1)}, f32[2,512,128,8]{2,1,3,0:T(8,128)}, u32[]{:S(2)}) copy-start(f32[2,512,128,8]{2,1,3,0:T(8,128)} %get-tuple-element.172) | copy-start | bytes 12582916 | tf_op jit(solution)/shard_map/while
  250.6 3.4 %copy-start.1 = (f32[2,512,128,8]{2,1,3,0:T(8,128)S(1)}, f32[2,512,128,8]{2,1,3,0:T(8,128)}, u32[]{:S(2)}) copy-start(f32[2,512,128,8]{2,1,3,0:T(8,128)} %get-tuple-element.172) | copy-start | bytes 12582916 | tf_op jit(solution)/shard_map/while
Sparse Core Ops, SparseCore 0:
  54.6 9.4 all-gather.4
  66.2 126.0 all-gather.6
  198.4 38.3 all-gather.8
where the time goes:
time: 264 us
  waiting for transfers between devices  181 us (69%)
  matrix products  18 us (7%)
  blocking collectives  17.5 us (7%)
  other arithmetic  14.7 us (6%)
  between operations  14 us (5%)
  starting transfers between devices  10.9 us (4%)
  local copies, waits for them, and re-layouts  7.43 us (3%)
    all_gather x1, waiting for transfers between devices, local(): lax.all_gather(kv_weight, 'dev', axis=0, tiled=True)  126 us
    all_to_all x1, waiting for transfers between devices, local(): lax.all_to_all(send_rows, 'dev', split_axis=0, concat_axis=0, tiled=True)  23.4 us
    all_gather x1, waiting for transfers between devices, local(): keys_part = lax.all_gather(kv, 'dev', axis=0, tiled=True)  17.5 us
    all_gather x1, blocking collectives, local(): key_pos = lax.all_gather(positions, 'dev', axis=0, tiled=True)  17.5 us
    all_gather x1, waiting for transfers between devices, local(): whole = lax.all_gather(embedded, 'pair', axis=1, tiled=True)  8.77 us
    all_to_all x1, starting transfers between devices, local(): lax.all_to_all(send_slots, 'dev', split_axis=0, concat_axis=0, tiled=True)  7.25 us
    reduce_sum x2, other arithmetic, score_block(): total = total * factor + jnp.sum(weights, axis=-1)  6.65 us
    dot_general x1, matrix products, local(): jnp.dot(normed, lax.all_gather(kv_weight, 'dev', axis=0, tiled=True), pre...  5.99 us
  transfers between devices with their start and end apart: 5, of which 5 were waited for; matrix products, arithmetic and copies ran while one was open for 3% of the time, Pallas kernels for 0%

commit v1 on v0

v1 whole, which is shorter than its diff:
```python
import functools

import jax
import jax.numpy as jnp
from jax import lax
from jax.experimental import pallas as pl
from jax.experimental.pallas import tpu as pltpu
from jax.sharding import PartitionSpec as P

MESH = pl.DeviceIdType.MESH
HD = 128
PAGE = 16
LANES = 128
F32 = jnp.float32
BF16 = jnp.bfloat16


def ring_position(d, n):
    z, x = d // 2, d % 2
    return z * (1 - x) + (n - 1 - z) * x


def ring_device(r, n):
    back = r // (n // 2)
    return (1 - back) * 2 * r + back * (2 * (n - 1 - r) + 1)


def kernel(
    n,
    cap,
    text_ref,
    vision_ref,
    dest_row_ref,
    dest_col_ref,
    slot_col_ref,
    pos_row_ref,
    pos_col_ref,
    gain_ref,
    weight_ref,
    bias_ref,
    query_ref,
    page_ref,
    out_ref,
    cache_ref,
    wbuf,
    vsend,
    vrecv,
    msend,
    mrecv,
    emb,
    nbuf,
    kvbuf,
    mask,
    local_sem,
    wsend_sem,
    wrecv_sem,
    ysend_sem,
    yrecv_sem,
    vsend_sem,
    vrecv_sem,
    msend_sem,
    mrecv_sem,
    psend_sem,
    precv_sem,
    ksend_sem,
    krecv_sem,
):
    rep = lax.axis_index("replica")
    me = lax.axis_index("dev")
    pair = lax.axis_index("pair")
    tok, half = text_ref.shape
    nvis = vision_ref.shape[0]
    shard = weight_ref.shape[0]
    own = shard // 3 // 16 * 16
    common = shard - 2 * own
    where = ring_position(me, n)

    def dev_id(d):
        return (rep, d, pair)

    other_pair = (rep, me, 1 - pair)
    other_rep = (1 - rep, me, pair)

    barrier = pltpu.get_barrier_semaphore()
    for off in range(1, n):
        pl.semaphore_signal(
            barrier, inc=1, device_id=dev_id(lax.rem(me + off, n)), device_id_type=MESH
        )
    pl.semaphore_signal(barrier, inc=1, device_id=other_pair, device_id_type=MESH)
    pl.semaphore_signal(barrier, inc=1, device_id=other_rep, device_id_type=MESH)
    local = pltpu.make_async_copy(weight_ref, wbuf.at[me], local_sem)
    local.start()
    pl.semaphore_wait(barrier, n + 1)

    def hop(buf, origin_ref, rows, way, k, send_sem, recv_sem):
        origin = ring_device(lax.rem(where - way * k + n, n), n)
        target = ring_device(lax.rem(where + way + n, n), n)
        source = buf.at[origin, rows] if k or origin_ref is None else origin_ref.at[rows]
        return pltpu.make_async_remote_copy(
            src_ref=source,
            dst_ref=buf.at[origin, rows],
            send_sem=send_sem,
            recv_sem=recv_sem,
            device_id=dev_id(target),
            device_id_type=MESH,
        )

    common_rows = pl.ds(0, common)
    own_rows = pl.ds(pl.multiple_of(common + rep * own, 16), own)
    streams = (
        (own_rows, 1, n // 2 - 1),
        (own_rows, -1, n // 2),
        (common_rows, 1, n // 2),
        (common_rows, -1, n // 2 - 1),
    )
    whops = [
        [
            hop(wbuf, weight_ref, rows, way, k, wsend_sem.at[i, k], wrecv_sem.at[i, k])
            for k in range(hops)
        ]
        for i, (rows, way, hops) in enumerate(streams)
    ]
    ycopies = []

    def ring_step(k):
        for i, (rows, way, hops) in enumerate(streams):
            if k > hops:
                continue
            if k:
                whops[i][k - 1].wait_recv()
            if k < hops:
                whops[i][k].start()
            if k and i < 2:
                origin = ring_device(lax.rem(where - way * k + n, n), n)
                index = k if way == 1 else n - k
                copy = pltpu.make_async_remote_copy(
                    src_ref=wbuf.at[origin, own_rows],
                    dst_ref=wbuf.at[origin, own_rows],
                    send_sem=ysend_sem.at[index],
                    recv_sem=yrecv_sem.at[index],
                    device_id=other_rep,
                    device_id_type=MESH,
                )
                copy.start()
                ycopies.append(copy)

    ring_step(0)

    dest_row, dest_col = dest_row_ref[...], dest_col_ref[...]
    row_i = lax.broadcasted_iota(jnp.int32, (nvis, nvis), 0)
    col_i = lax.broadcasted_iota(jnp.int32, (nvis, nvis), 1)
    same = dest_row == dest_col
    rank_col = jnp.sum(
        jnp.where(same & (col_i < row_i), 1.0, 0.0), axis=1, keepdims=True
    ).astype(jnp.int32)
    rank_row = jnp.sum(
        jnp.where(same & (row_i < col_i), 1.0, 0.0), axis=0, keepdims=True
    ).astype(jnp.int32)
    order = dest_row * cap + rank_row
    per = LANES // cap
    lane = lax.broadcasted_iota(jnp.int32, (nvis, LANES), 1)
    place = dest_col * LANES + lax.rem(me, per) * cap + rank_col
    slots = slot_col_ref[...] + 1
    for d in range(n):
        msend[d, 0:1, :] = jnp.sum(
            jnp.where(place == d * LANES + lane, slots.astype(F32), 0.0), axis=0, keepdims=True
        ).astype(jnp.int32)
        msend[d, 1:2, :] = pos_row_ref[...]
    vision = vision_ref[...]
    for block in range(n * cap // LANES):
        select = order == block * LANES + lax.broadcasted_iota(jnp.int32, (LANES, nvis), 0)
        vsend[pl.ds(block * LANES, LANES), :] = jnp.dot(
            jnp.where(select, 1.0, 0.0).astype(BF16), vision, preferred_element_type=F32
        ).astype(BF16)

    def cap_rows(d):
        return pl.ds(pl.multiple_of(d * cap, 16), cap)

    vcopies = []
    for off in range(1, n):
        target = lax.rem(me + off, n)
        for src, dst, ssem, rsem in (
            (msend.at[target], mrecv.at[me], msend_sem, mrecv_sem),
            (vsend.at[cap_rows(target)], vrecv.at[cap_rows(me)], vsend_sem, vrecv_sem),
        ):
            copy = pltpu.make_async_remote_copy(
                src_ref=src,
                dst_ref=dst,
                send_sem=ssem.at[off],
                recv_sem=rsem.at[off],
                device_id=dev_id(target),
                device_id_type=MESH,
            )
            copy.start()
            vcopies.append(copy)
    mrecv[pl.ds(me, 1)] = msend[pl.ds(me, 1)]
    vrecv[cap_rows(me), :] = vsend[cap_rows(me), :]

    ring_step(1)

    for copy in vcopies:
        copy.wait_recv()
    added = jnp.zeros((tok, half), F32)
    for g in range(n * cap // LANES):
        slot_row = sum([mrecv[s, 0:1, :] for s in range(g * per, (g + 1) * per)])
        hit = lax.broadcasted_iota(jnp.int32, (tok, LANES), 0) + 1 == slot_row
        added += jnp.dot(
            jnp.where(hit, 1.0, 0.0).astype(BF16),
            vrecv[pl.ds(g * LANES, LANES), :],
            preferred_element_type=F32,
        )
    emb[pl.ds(pair, 1)] = (text_ref[...].astype(F32) + added).astype(BF16)[None]
    pair_copy = pltpu.make_async_remote_copy(
        src_ref=emb.at[pair],
        dst_ref=emb.at[pair],
        send_sem=psend_sem,
        recv_sem=precv_sem,
        device_id=other_pair,
        device_id_type=MESH,
    )
    pair_copy.start()

    for s in range(n):
        mask[:, s * tok : (s + 1) * tok] = jnp.where(
            mrecv[s, 1:2, :] <= pos_col_ref[...], 0.0, -1e30
        )

    ring_step(2)

    pair_copy.wait_recv()
    squares = jnp.zeros((tok, 1), F32)
    for d in range(n):
        floats = emb[d // (n // 2), :, pl.ds(d % (n // 2) * shard, shard)].astype(F32)
        squares += jnp.sum(floats * floats, axis=1, keepdims=True)
    scale = lax.rsqrt(squares / (2 * half) + 1e-6)
    for d in range(n):
        floats = emb[d // (n // 2), :, pl.ds(d % (n // 2) * shard, shard)].astype(F32)
        gain = gain_ref[:, pl.ds(d * shard, shard)].astype(F32)
        nbuf[d] = (floats * scale * gain).astype(BF16)

    for k in range(3, n // 2 + 1):
        ring_step(k)
    for copy in ycopies:
        copy.wait_recv()
    local.wait()
    acc = jnp.zeros((tok, weight_ref.shape[1]), F32)
    for d in range(n):
        acc += jnp.dot(nbuf[d], wbuf[d], preferred_element_type=F32)
    kv = (acc + bias_ref[...].astype(F32)).astype(BF16)
    kvbuf[pl.ds(me, 1)] = kv[None]

    first, second = pl.ds(0, tok // 2), pl.ds(tok // 2, tok // 2)
    kstreams = (
        (first, 1, n // 2),
        (first, -1, n // 2 - 1),
        (second, 1, n // 2 - 1),
        (second, -1, n // 2),
    )
    khops = [
        [
            hop(kvbuf, None, rows, way, k, ksend_sem.at[i, k], krecv_sem.at[i, k])
            for k in range(hops)
        ]
        for i, (rows, way, hops) in enumerate(kstreams)
    ]
    for k in range(n // 2 + 1):
        for i, (rows, way, hops) in enumerate(kstreams):
            if k > hops:
                continue
            if k:
                khops[i][k - 1].wait_recv()
            if k < hops:
                khops[i][k].start()
        if k == 0:
            line = lax.broadcasted_iota(jnp.int32, (tok, tok), 1)
            pick = page_ref[...] == line
            cache_ref[...] = jnp.dot(
                jnp.where(pick, 1.0, 0.0).astype(BF16), kv, preferred_element_type=F32
            ).astype(BF16)

    heads = kv.shape[1] // (2 * HD)
    group = query_ref.shape[1] // (HD * heads)
    for head in range(heads):
        keys = kvbuf[:, :, head * 2 * HD : head * 2 * HD + HD].reshape(n * tok, HD)
        values = kvbuf[:, :, head * 2 * HD + HD : (head + 1) * 2 * HD].reshape(n * tok, HD)

        def one(j, carry, head=head, keys=keys, values=values):
            column = pl.ds(pl.multiple_of((head * group + j) * HD, HD), HD)
            scores = lax.dot_general(
                query_ref[:, column], keys, (((1,), (1,)), ((), ())), preferred_element_type=F32
            )
            scores = scores * HD ** (-0.5) + mask[...]
            peak = jnp.max(scores, axis=1, keepdims=True)
            weights = jnp.exp(scores - peak)
            total = jnp.sum(weights, axis=1, keepdims=True)
            mixed = jnp.dot(weights.astype(BF16), values, preferred_element_type=F32)
            out_ref[:, column] = (mixed / total).astype(BF16)
            return carry

        lax.fori_loop(0, group, one, 0, unroll=2 if n <= 8 else 1)

    for hops in whops + khops:
        for copy in hops:
            copy.wait_send()
    for copy in ycopies + vcopies + [pair_copy]:
        copy.wait_send()


def local(
    text_rows,
    vision_rows,
    vision_device,
    vision_slot,
    positions,
    norm_gain,
    kv_weight,
    kv_bias,
    queries,
    page_table,
):
    n = lax.axis_size("dev")
    tok, half = text_rows.shape
    nvis = vision_rows.shape[0]
    shard, columns = kv_weight.shape
    cap = max(16, 2 * nvis // n)
    pages = page_table.shape[1]
    page_rows = (
        page_table.reshape(pages, 1) * PAGE + jnp.arange(PAGE, dtype=jnp.int32)[None, :]
    ).reshape(tok, 1)
    dma = pltpu.SemaphoreType.DMA
    attended, cache = pl.pallas_call(
        functools.partial(kernel, n, cap),
        out_shape=(
            jax.ShapeDtypeStruct(queries.shape, BF16),
            jax.ShapeDtypeStruct((tok, columns), BF16),
        ),
        in_specs=[pl.BlockSpec(memory_space=pltpu.VMEM)] * 12,
        out_specs=(pl.BlockSpec(memory_space=pltpu.VMEM),) * 2,
        scratch_shapes=[
            pltpu.VMEM((n, shard, columns), BF16),
            pltpu.VMEM((n * cap, half), BF16),
            pltpu.VMEM((n * cap, half), BF16),
            pltpu.VMEM((n, 8, LANES), jnp.int32),
            pltpu.VMEM((n, 8, LANES), jnp.int32),
            pltpu.VMEM((2, tok, half), BF16),
            pltpu.VMEM((n, tok, shard), BF16),
            pltpu.VMEM((n, tok, columns), BF16),
            pltpu.VMEM((tok, n * tok), F32),
            dma,
            dma((4, n)),
            dma((4, n)),
            dma((n,)),
            dma((n,)),
            dma((n,)),
            dma((n,)),
            dma((n,)),
            dma((n,)),
            dma,
            dma,
            dma((4, n)),
            dma((4, n)),
        ],
        compiler_params=pltpu.CompilerParams(
            collective_id=0, has_side_effects=True, vmem_limit_bytes=60 * 1024 * 1024
        ),
    )(
        text_rows,
        vision_rows,
        vision_device.reshape(1, nvis),
        vision_device,
        vision_slot.reshape(nvis, 1),
        positions.reshape(1, tok),
        positions.reshape(tok, 1),
        norm_gain.reshape(1, -1),
        kv_weight,
        kv_bias.reshape(1, columns),
        queries,
        page_rows,
    )
    return (attended, cache.reshape(pages, PAGE, columns))


def solution(mesh):
    placed = (
        P(("replica", "dev"), "pair"),
        P(("replica", "dev"), "pair"),
        P(("replica", "dev"), None),
        P(("replica", "dev")),
        P(("replica", "dev")),
        P(),
        P("dev", "pair"),
        P("pair"),
        P(("replica", "dev"), "pair"),
        P(("replica", "dev"), None),
    )
    return jax.shard_map(
        local,
        mesh=mesh,
        in_specs=placed,
        out_specs=(P(("replica", "dev"), "pair"), P(("replica", "dev"), None, "pair")),
        check_vma=False,
    )
```

time: 264 us -> 129 us (0.49)
  waiting for transfers between devices: 181 us -> 0 us
  Pallas kernels: 0 us -> 119 us
  matrix products: 18 us -> 0 us
  blocking collectives: 17.5 us -> 0 us
  other arithmetic: 14.7 us -> 0.07 us
  between operations: 14 us -> 0.66 us
  starting transfers between devices: 10.9 us -> 0 us
    all_gather x3 -> x0, waiting for transfers between devices: 152 us -> none  [the longest x1 126 us: local(): lax.all_gather(kv_weight, 'dev', axis=0, tiled=True)]
    pallas_call x0 -> x1, Pallas kernels: none -> 119 us  [local(): pl.pallas_call(functools.partial(kernel, n, cap), out_shape=(jax.ShapeDty...]
    all_to_all x2 -> x0, waiting for transfers between devices: 28.2 us -> none  [the longest x1 23.4 us: local(): lax.all_to_all(send_rows, 'dev', split_axis=0, concat_axis=0, tiled=True)]
    dot_general x7 -> x0, matrix products: 18 us -> none  [the longest x1 5.99 us: local(): jnp.dot(normed, lax.all_gather(kv_weight, 'dev', axis=0, tiled=True), pre...]
    all_gather x1 -> x0, blocking collectives: 17.5 us -> none  [local(): key_pos = lax.all_gather(positions, 'dev', axis=0, tiled=True)]
    all_to_all x2 -> x0, starting transfers between devices: 10.8 us -> none  [the longest x1 7.25 us: local(): lax.all_to_all(send_slots, 'dev', split_axis=0, concat_axis=0, tiled=True)]
    reduce_sum x4 -> x0, other arithmetic: 9.56 us -> none  [the longest x2 6.65 us: score_block(): total = total * factor + jnp.sum(weights, axis=-1)]
    unnamed x17, local copies, waits for them, and re-layouts: 1.54 us -> 5.24 us
  transfers between devices with their start and end apart: 5 -> 0, of which waited for: 5 -> 0; matrix products, arithmetic and copies ran while one was open for 3% -> 0% of each run, Pallas kernels for 0% -> 0%
where the time goes in v1:
time: 129 us; the launch traced here: 128 us
  Pallas kernels  119 us (92%)
  local copies, waits for them, and re-layouts  8.6 us (7%)
    pallas_call x1, Pallas kernels, local(): pl.pallas_call(functools.partial(kernel, n, cap), out_shape=(jax.ShapeDty...  119 us
    unnamed x17, local copies, waits for them, and re-layouts  5.24 us

profile of v1, /device:TPU:0, one launch (start us, length us, event | category | flops | bytes accessed | tf_op | source)
XLA Modules:
  0.0 128.4 jit_solution(2574254412414991328)
XLA Ops:
  0.6 0.0 copy-start.6
  0.6 0.6 copy-done.6
  1.3 0.0 copy-start.4
  1.3 0.7 copy-done.4
  2.0 0.6 reshape.63.bias_ref
  2.6 0.0 copy-start.5
  2.6 0.1 iota_add_fusion
  2.6 0.6 copy-done.5
  3.2 0.0 copy-start.1
  3.2 0.7 copy.13.slot_col_ref
  3.9 0.0 copy-done.1
  3.9 0.0 copy-start.2
  3.9 0.6 reshape.62.gain_ref
  4.6 0.0 copy-done.2
  4.6 0.7 copy.12.dest_col_ref
  5.3 0.0 copy-start.3
  5.3 0.7 add.27.page_ref
  6.0 0.0 copy-done.3
  6.0 0.7 copy.14.pos_col_ref
  6.7 119.0 %shard_map.113 = (bf16[128,2048]{1,0:T(8,128)(2,1)}, bf16[128,512]{1,0:T(8,128)(2,1)}) custom-call(bf16[128,4096]{1,0:T(8,128)(2,1)} %text_ref.1, bf16[64,4096]{1,0:T(8,128)(2,1)} %vision_ref.1, s32[1,64]{1,0:T(1,128)} %bitcast.8, s32[64,1]{1,0:T(8,128)} %copy.12.dest_col_ref, s32[64,1]{1,0:T(8,128)} %copy.13.slot_col_ref, s32[1,128]{1,0:T(1,128)} %bitcast.9, ...), custom_call_target="tpu_custom_call" | custom-call | tf_op jit(solution)/shard_map/pallas_call | solution.py:331
  125.8 0.0 copy-start
  125.8 1.9 %copy.18 = bf16[128,2048]{1,0:T(8,128)(2,1)} copy(bf16[128,2048]{1,0:T(8,128)(2,1)} %get-tuple-element.8) | data formatting | bytes 1048576
  127.7 0.0 copy-done
  127.7 0.7 copy.19
  (1 shorter events, 0.0 us)
Async XLA Ops:
  0.6 0.7 copy-start.6
  1.3 0.7 copy-start.4
  2.6 0.7 copy-start.5
  3.2 0.7 copy-start.1
  3.9 0.7 copy-start.2
  5.3 0.7 copy-start.3
  125.8 1.9 %copy-start = (bf16[128,512]{1,0:T(8,128)(2,1)S(1)}, bf16[128,512]{1,0:T(8,128)(2,1)}, u32[]{:S(2)}) copy-start(bf16[128,512]{1,0:T(8,128)(2,1)} %get-tuple-element.5) | copy-start | bytes 393220

commit v2 on v1

--- a/solution.py
+++ b/solution.py
@@ -30,16 +30,14 @@
     cap,
     text_ref,
     vision_ref,
-    dest_row_ref,
-    dest_col_ref,
-    slot_col_ref,
-    pos_row_ref,
-    pos_col_ref,
+    dest_ref,
+    slot_ref,
+    pos_ref,
+    page_ref,
     gain_ref,
+    bias_ref,
     weight_ref,
-    bias_ref,
     query_ref,
-    page_ref,
     out_ref,
     cache_ref,
     wbuf,
@@ -71,7 +69,7 @@
     tok, half = text_ref.shape
     nvis = vision_ref.shape[0]
     shard = weight_ref.shape[0]
-    own = shard // 3 // 16 * 16
+    own = shard * 2 // 5 // 16 * 16
     common = shard - 2 * own
     where = ring_position(me, n)
 
@@ -105,13 +103,24 @@
             device_id_type=MESH,
         )
 
-    common_rows = pl.ds(0, common)
-    own_rows = pl.ds(pl.multiple_of(common + rep * own, 16), own)
+    own_at = common + rep * own
+    own_cut = (own // 2 + 15) // 16 * 16
+    common_cut = (common // 2 + 15) // 16 * 16
+    own_parts = (
+        pl.ds(pl.multiple_of(own_at, 16), own_cut),
+        pl.ds(pl.multiple_of(own_at + own_cut, 16), own - own_cut),
+    )
+    common_parts = (pl.ds(0, common_cut), pl.ds(common_cut, common - common_cut))
+    far = n // 2
     streams = (
-        (own_rows, 1, n // 2 - 1),
-        (own_rows, -1, n // 2),
-        (common_rows, 1, n // 2),
-        (common_rows, -1, n // 2 - 1),
+        (own_parts[0], 1, far - 1),
+        (own_parts[1], -1, far - 1),
+        (own_parts[1], 1, far),
+        (own_parts[0], -1, far),
+        (common_parts[0], 1, far),
+        (common_parts[1], -1, far),
+        (common_parts[1], 1, far - 1),
+        (common_parts[0], -1, far - 1),
     )
     whops = [
         [
@@ -120,7 +129,7 @@
         ]
         for i, (rows, way, hops) in enumerate(streams)
     ]
-    ycopies = []
+    ycopies = {}
 
     def ring_step(k):
         for i, (rows, way, hops) in enumerate(streams):
@@ -130,23 +139,45 @@
                 whops[i][k - 1].wait_recv()
             if k < hops:
                 whops[i][k].start()
-            if k and i < 2:
+            if k and i < 4:
                 origin = ring_device(lax.rem(where - way * k + n, n), n)
                 index = k if way == 1 else n - k
+                part = (0, 1, 1, 0)[i]
                 copy = pltpu.make_async_remote_copy(
-                    src_ref=wbuf.at[origin, own_rows],
-                    dst_ref=wbuf.at[origin, own_rows],
-                    send_sem=ysend_sem.at[index],
-                    recv_sem=yrecv_sem.at[index],
+                    src_ref=wbuf.at[origin, rows],
+                    dst_ref=wbuf.at[origin, rows],
+                    send_sem=ysend_sem.at[part, index],
+                    recv_sem=yrecv_sem.at[part, index],
                     device_id=other_rep,
                     device_id_type=MESH,
                 )
                 copy.start()
-                ycopies.append(copy)
+                ycopies[part, index] = copy
 
     ring_step(0)
 
-    dest_row, dest_col = dest_row_ref[...], dest_col_ref[...]
+    def column(line, size):
+        diagonal = lax.broadcasted_iota(jnp.int32, (size, size), 0) == lax.broadcasted_iota(
+            jnp.int32, (size, size), 1
+        )
+        return jnp.sum(
+            jnp.where(diagonal, line.astype(F32), 0.0), axis=1, keepdims=True
+        ).astype(jnp.int32)
+
+    dest_row = dest_ref[...]
+    dest_col = column(dest_row, nvis)
+    pos_row = pos_ref[...]
+    pos_col = column(pos_row, tok)
+    pages = page_ref.shape[1]
+    row_of = lax.broadcasted_iota(jnp.int32, (tok, pages), 0)
+    page_of = lax.broadcasted_iota(jnp.int32, (tok, pages), 1)
+    first_row = page_of * PAGE
+    in_page = (row_of >= first_row) & (row_of < first_row + PAGE)
+    page_col = jnp.sum(
+        jnp.where(in_page, (page_ref[...] * PAGE + row_of - first_row).astype(F32), 0.0),
+        axis=1,
+        keepdims=True,
+    ).astype(jnp.int32)
     row_i = lax.broadcasted_iota(jnp.int32, (nvis, nvis), 0)
     col_i = lax.broadcasted_iota(jnp.int32, (nvis, nvis), 1)
     same = dest_row == dest_col
@@ -160,12 +191,12 @@
     per = LANES // cap
     lane = lax.broadcasted_iota(jnp.int32, (nvis, LANES), 1)
     place = dest_col * LANES + lax.rem(me, per) * cap + rank_col
-    slots = slot_col_ref[...] + 1
+    slots = column(slot_ref[...], nvis) + 1
     for d in range(n):
         msend[d, 0:1, :] = jnp.sum(
             jnp.where(place == d * LANES + lane, slots.astype(F32), 0.0), axis=0, keepdims=True
         ).astype(jnp.int32)
-        msend[d, 1:2, :] = pos_row_ref[...]
+        msend[d, 1:2, :] = pos_row
     vision = vision_ref[...]
     for block in range(n * cap // LANES):
         select = order == block * LANES + lax.broadcasted_iota(jnp.int32, (LANES, nvis), 0)
@@ -197,6 +228,8 @@
     vrecv[cap_rows(me), :] = vsend[cap_rows(me), :]
 
     ring_step(1)
+    for k in range(2, far - 1):
+        ring_step(k)
 
     for copy in vcopies:
         copy.wait_recv()
@@ -222,10 +255,10 @@
 
     for s in range(n):
         mask[:, s * tok : (s + 1) * tok] = jnp.where(
-            mrecv[s, 1:2, :] <= pos_col_ref[...], 0.0, -1e30
+            mrecv[s, 1:2, :] <= pos_col, 0.0, -1e30
         )
 
-    ring_step(2)
+    ring_step(far - 1)
 
     pair_copy.wait_recv()
     squares = jnp.zeros((tok, 1), F32)
@@ -238,14 +271,21 @@
         gain = gain_ref[:, pl.ds(d * shard, shard)].astype(F32)
         nbuf[d] = (floats * scale * gain).astype(BF16)
 
-    for k in range(3, n // 2 + 1):
-        ring_step(k)
-    for copy in ycopies:
-        copy.wait_recv()
     local.wait()
-    acc = jnp.zeros((tok, weight_ref.shape[1]), F32)
-    for d in range(n):
-        acc += jnp.dot(nbuf[d], wbuf[d], preferred_element_type=F32)
+    acc = jnp.dot(nbuf[me], wbuf[me], preferred_element_type=F32)
+
+    def projected(total, steps):
+        for step in steps:
+            for part in range(2):
+                ycopies[part, step].wait_recv()
+            d = ring_device(lax.rem(where - step + n, n), n)
+            total += jnp.dot(nbuf[d], wbuf[d], preferred_element_type=F32)
+        return total
+
+    near = [k for step in range(1, far - 1) for k in (step, n - step)]
+    acc = projected(acc, near)
+    ring_step(far)
+    acc = projected(acc, (far - 1, far + 1, far))
     kv = (acc + bias_ref[...].astype(F32)).astype(BF16)
     kvbuf[pl.ds(me, 1)] = kv[None]
 
@@ -273,7 +313,7 @@
                 khops[i][k].start()
         if k == 0:
             line = lax.broadcasted_iota(jnp.int32, (tok, tok), 1)
-            pick = page_ref[...] == line
+            pick = page_col == line
             cache_ref[...] = jnp.dot(
                 jnp.where(pick, 1.0, 0.0).astype(BF16), kv, preferred_element_type=F32
             ).astype(BF16)
@@ -285,16 +325,16 @@
         values = kvbuf[:, :, head * 2 * HD + HD : (head + 1) * 2 * HD].reshape(n * tok, HD)
 
         def one(j, carry, head=head, keys=keys, values=values):
-            column = pl.ds(pl.multiple_of((head * group + j) * HD, HD), HD)
+            span = pl.ds(pl.multiple_of((head * group + j) * HD, HD), HD)
             scores = lax.dot_general(
-                query_ref[:, column], keys, (((1,), (1,)), ((), ())), preferred_element_type=F32
+                query_ref[:, span], keys, (((1,), (1,)), ((), ())), preferred_element_type=F32
             )
             scores = scores * HD ** (-0.5) + mask[...]
             peak = jnp.max(scores, axis=1, keepdims=True)
             weights = jnp.exp(scores - peak)
             total = jnp.sum(weights, axis=1, keepdims=True)
             mixed = jnp.dot(weights.astype(BF16), values, preferred_element_type=F32)
-            out_ref[:, column] = (mixed / total).astype(BF16)
+            out_ref[:, span] = (mixed / total).astype(BF16)
             return carry
 
         lax.fori_loop(0, group, one, 0, unroll=2 if n <= 8 else 1)
@@ -302,7 +342,7 @@
     for hops in whops + khops:
         for copy in hops:
             copy.wait_send()
-    for copy in ycopies + vcopies + [pair_copy]:
+    for copy in list(ycopies.values()) + vcopies + [pair_copy]:
         copy.wait_send()
 
 
@@ -324,9 +364,6 @@
     shard, columns = kv_weight.shape
     cap = max(16, 2 * nvis // n)
     pages = page_table.shape[1]
-    page_rows = (
-        page_table.reshape(pages, 1) * PAGE + jnp.arange(PAGE, dtype=jnp.int32)[None, :]
-    ).reshape(tok, 1)
     dma = pltpu.SemaphoreType.DMA
     attended, cache = pl.pallas_call(
         functools.partial(kernel, n, cap),
@@ -334,7 +371,7 @@
             jax.ShapeDtypeStruct(queries.shape, BF16),
             jax.ShapeDtypeStruct((tok, columns), BF16),
         ),
-        in_specs=[pl.BlockSpec(memory_space=pltpu.VMEM)] * 12,
+        in_specs=[pl.BlockSpec(memory_space=pltpu.VMEM)] * 10,
         out_specs=(pl.BlockSpec(memory_space=pltpu.VMEM),) * 2,
         scratch_shapes=[
             pltpu.VMEM((n, shard, columns), BF16),
@@ -347,10 +384,10 @@
             pltpu.VMEM((n, tok, columns), BF16),
             pltpu.VMEM((tok, n * tok), F32),
             dma,
-            dma((4, n)),
-            dma((4, n)),
-            dma((n,)),
-            dma((n,)),
+            dma((8, n)),
+            dma((8, n)),
+            dma((2, n)),
+            dma((2, n)),
             dma((n,)),
             dma((n,)),
             dma((n,)),
@@ -367,15 +404,13 @@
         text_rows,
         vision_rows,
         vision_device.reshape(1, nvis),
-        vision_device,
-        vision_slot.reshape(nvis, 1),
+        vision_slot.reshape(1, nvis),
         positions.reshape(1, tok),
-        positions.reshape(tok, 1),
+        page_table,
         norm_gain.reshape(1, -1),
+        kv_bias.reshape(1, -1),
         kv_weight,
-        kv_bias.reshape(1, columns),
         queries,
-        page_rows,
     )
     return (attended, cache.reshape(pages, PAGE, columns))
 

time: 129 us -> 126 us (0.977)
  local copies, waits for them, and re-layouts: 8.6 us -> 5.18 us
    unnamed x17 -> x6, local copies, waits for them, and re-layouts: 5.24 us -> 3.25 us
    reshape x3 -> x1, local copies, waits for them, and re-layouts: 2.03 us -> 0.58 us  [local(): kv_bias.reshape(1, -1)]
where the time goes in v2:
time: 126 us
  Pallas kernels  120 us (95%)
  local copies, waits for them, and re-layouts  5.18 us (4%)
    pallas_call x1, Pallas kernels, local(): pl.pallas_call(functools.partial(kernel, n, cap), out_shape=(jax.ShapeDty...  120 us
    unnamed x6, local copies, waits for them, and re-layouts  3.25 us

profile of v2, /device:TPU:0, one launch (start us, length us, event | category | flops | bytes accessed | tf_op | source)
XLA Modules:
  0.0 125.7 jit_solution(6404754430145240125)
XLA Ops:
  0.6 0.0 copy-start.1
  0.6 0.7 copy-done.1
  1.3 0.6 reshape.26.bias_ref
  1.9 1.3 %reshape.25.gain_ref = bf16[1,8192]{1,0:T(2,128)(2,1)} reshape(bf16[8192]{0:T(1024)(128)(2,1)} %param.15) | data formatting | bytes 32768 | tf_op jit(solution)/shard_map/reshape | solution.py:410
  3.2 119.9 %shard_map.113 = (bf16[128,2048]{1,0:T(8,128)(2,1)}, bf16[128,512]{1,0:T(8,128)(2,1)}) custom-call(bf16[128,4096]{1,0:T(8,128)(2,1)} %text_ref.1, bf16[64,4096]{1,0:T(8,128)(2,1)} %vision_ref.1, s32[1,64]{1,0:T(1,128)} %bitcast.5, s32[1,64]{1,0:T(1,128)} %bitcast.6, s32[1,128]{1,0:T(1,128)} %bitcast.7, s32[1,8]{1,0:T(1,128)} %page_ref.1, ...), custom_call_target="tpu_custom_call" | custom-call | tf_op jit(solution)/shard_map/pallas_call | solution.py:368
  123.1 0.0 copy-start
  123.1 1.9 %copy.14 = bf16[128,2048]{1,0:T(8,128)(2,1)} copy(bf16[128,2048]{1,0:T(8,128)(2,1)} %get-tuple-element.8) | data formatting | bytes 1048576
  125.1 0.0 copy-done
  125.1 0.7 copy.15
Async XLA Ops:
  0.6 0.7 copy-start.1
  123.1 1.9 %copy-start = (bf16[128,512]{1,0:T(8,128)(2,1)S(1)}, bf16[128,512]{1,0:T(8,128)(2,1)}, u32[]{:S(2)}) copy-start(bf16[128,512]{1,0:T(8,128)(2,1)} %get-tuple-element.5) | copy-start | bytes 393220

commit v3 on v2

--- a/solution.py
+++ b/solution.py
@@ -69,7 +69,7 @@
     tok, half = text_ref.shape
     nvis = vision_ref.shape[0]
     shard = weight_ref.shape[0]
-    own = shard * 2 // 5 // 16 * 16
+    own = shard // 3 // 16 * 16
     common = shard - 2 * own
     where = ring_position(me, n)
 

time: 126 us -> 120 us (0.952)
  Pallas kernels: 120 us -> 114 us
    pallas_call x1, Pallas kernels: 120 us -> 114 us  [local(): pl.pallas_call(functools.partial(kernel, n, cap), out_shape=(jax.ShapeDty...]
where the time goes in v3:
time: 120 us
  Pallas kernels  114 us (95%)
  local copies, waits for them, and re-layouts  5.18 us (4%)
    pallas_call x1, Pallas kernels, local(): pl.pallas_call(functools.partial(kernel, n, cap), out_shape=(jax.ShapeDty...  114 us
    unnamed x6, local copies, waits for them, and re-layouts  3.25 us

profile of v3, /device:TPU:0, one launch (start us, length us, event | category | flops | bytes accessed | tf_op | source)
XLA Modules:
  0.0 119.8 jit_solution(14088050355356242612)
XLA Ops:
  0.6 0.0 copy-start.1
  0.6 0.7 copy-done.1
  1.3 0.6 reshape.26.bias_ref
  1.9 1.3 %reshape.25.gain_ref = bf16[1,8192]{1,0:T(2,128)(2,1)} reshape(bf16[8192]{0:T(1024)(128)(2,1)} %param.15) | data formatting | bytes 32768 | tf_op jit(solution)/shard_map/reshape | solution.py:410
  3.2 113.9 %shard_map.113 = (bf16[128,2048]{1,0:T(8,128)(2,1)}, bf16[128,512]{1,0:T(8,128)(2,1)}) custom-call(bf16[128,4096]{1,0:T(8,128)(2,1)} %text_ref.1, bf16[64,4096]{1,0:T(8,128)(2,1)} %vision_ref.1, s32[1,64]{1,0:T(1,128)} %bitcast.5, s32[1,64]{1,0:T(1,128)} %bitcast.6, s32[1,128]{1,0:T(1,128)} %bitcast.7, s32[1,8]{1,0:T(1,128)} %page_ref.1, ...), custom_call_target="tpu_custom_call" | custom-call | tf_op jit(solution)/shard_map/pallas_call | solution.py:368
  117.2 0.0 copy-start
  117.2 1.9 %copy.14 = bf16[128,2048]{1,0:T(8,128)(2,1)} copy(bf16[128,2048]{1,0:T(8,128)(2,1)} %get-tuple-element.8) | data formatting | bytes 1048576
  119.1 0.0 copy-done
  119.1 0.7 copy.15
Async XLA Ops:
  0.6 0.7 copy-start.1
  117.2 1.9 %copy-start = (bf16[128,512]{1,0:T(8,128)(2,1)S(1)}, bf16[128,512]{1,0:T(8,128)(2,1)}, u32[]{:S(2)}) copy-start(bf16[128,512]{1,0:T(8,128)(2,1)} %get-tuple-element.5) | copy-start | bytes 393220

commit v4 on v3

--- a/solution.py
+++ b/solution.py
@@ -337,7 +337,7 @@
             out_ref[:, span] = (mixed / total).astype(BF16)
             return carry
 
-        lax.fori_loop(0, group, one, 0, unroll=2 if n <= 8 else 1)
+        lax.fori_loop(0, group, one, 0, unroll=8 if n <= 8 else 1)
 
     for hops in whops + khops:
         for copy in hops:

time: 120 us -> 119 us (level)
  no operation moved by 1% of the time
where the time goes in v4:
time: 119 us
  Pallas kernels  113 us (95%)
  local copies, waits for them, and re-layouts  5.18 us (4%)
    pallas_call x1, Pallas kernels, local(): pl.pallas_call(functools.partial(kernel, n, cap), out_shape=(jax.ShapeDty...  113 us
    unnamed x6, local copies, waits for them, and re-layouts  3.25 us

profile of v4, /device:TPU:0, one launch (start us, length us, event | category | flops | bytes accessed | tf_op | source)
XLA Modules:
  0.0 118.6 jit_solution(15523563402289035937)
XLA Ops:
  0.6 0.0 copy-start.1
  0.6 0.7 copy-done.1
  1.3 0.6 reshape.26.bias_ref
  1.9 1.3 %reshape.25.gain_ref = bf16[1,8192]{1,0:T(2,128)(2,1)} reshape(bf16[8192]{0:T(1024)(128)(2,1)} %param.15) | data formatting | bytes 32768 | tf_op jit(solution)/shard_map/reshape | solution.py:410
  3.2 112.7 %shard_map.113 = (bf16[128,2048]{1,0:T(8,128)(2,1)}, bf16[128,512]{1,0:T(8,128)(2,1)}) custom-call(bf16[128,4096]{1,0:T(8,128)(2,1)} %text_ref.1, bf16[64,4096]{1,0:T(8,128)(2,1)} %vision_ref.1, s32[1,64]{1,0:T(1,128)} %bitcast.5, s32[1,64]{1,0:T(1,128)} %bitcast.6, s32[1,128]{1,0:T(1,128)} %bitcast.7, s32[1,8]{1,0:T(1,128)} %page_ref.1, ...), custom_call_target="tpu_custom_call" | custom-call | tf_op jit(solution)/shard_map/pallas_call | solution.py:368
  116.0 0.0 copy-start
  116.0 1.9 %copy.14 = bf16[128,2048]{1,0:T(8,128)(2,1)} copy(bf16[128,2048]{1,0:T(8,128)(2,1)} %get-tuple-element.8) | data formatting | bytes 1048576
  117.9 0.0 copy-done
  117.9 0.7 copy.15
Async XLA Ops:
  0.6 0.7 copy-start.1
  116.0 1.9 %copy-start = (bf16[128,512]{1,0:T(8,128)(2,1)S(1)}, bf16[128,512]{1,0:T(8,128)(2,1)}, u32[]{:S(2)}) copy-start(bf16[128,512]{1,0:T(8,128)(2,1)} %get-tuple-element.5) | copy-start | bytes 393220
